TPU v7x, 32 devices: a whole 2x2x4 slice. The times are simulated.
32 devices in a mesh: pipe: 2 (over core), ctx: 4 (over z), dp: 4 (over y, x).
Axes of the slice: x: 2, y: 2, z: 4, core: 2. Of those that a mesh axis runs over, the one named last changes fastest.
Arguments:
- queries: bfloat16 [2, 4, 512, 2048], P('pipe', 'dp', 'ctx'), may hold values from -6 to 6
- keys: bfloat16 [2, 4, 512, 2048], P('pipe', 'dp', 'ctx'), may hold values from -6 to 6
- values: bfloat16 [2, 4, 512, 2048], P('pipe', 'dp', 'ctx'), may hold values from -6 to 6
- upstream: bfloat16 [2, 4, 512, 2048], P('pipe', 'dp', 'ctx'), may hold values from -6 to 6
- gain: float32 [2, 2048], P('pipe', 'ctx'), may hold values from 0.1 to 1.9
Outputs:
- query_grad: bfloat16 [2, 4, 512, 2048], P('pipe', 'dp', 'ctx')
- key_grad: bfloat16 [2, 4, 512, 2048], P('pipe', 'dp', 'ctx')
- value_grad: bfloat16 [2, 4, 512, 2048], P('pipe', 'dp', 'ctx')
- gain_grad: float32 [2, 2048], P('pipe', 'ctx')
All inputs are finite; a program needn't handle non-finite values.
Results may differ from a plain program's by a relative error of at most 0.007.
Values may be sent and summed in bfloat16 or wider, within the bound.
A program may use at most 64 MiB of HBM per device.

v0:
```python
import functools

import jax
import jax.numpy as jnp
from jax import lax
from jax.experimental import pallas as pl
from jax.experimental.pallas import tpu as pltpu
from jax.sharding import PartitionSpec as P

HEAD_DIM = 128
STRETCH = 128
WINDOW = 512


def shifted_2(array, axis, by):
    devices = lax.axis_size(axis)
    return lax.ppermute(array, axis, [(i, (i + by) % devices) for i in range(devices)])


def contract(form, left, right):
    return jnp.einsum(form, left, right, preferred_element_type=jnp.float32)


def shifted(tensor, amount):
    length = tensor.shape[0]
    amount = min(amount, length)
    filler = jnp.zeros((amount,) + tensor.shape[1:], tensor.dtype)
    return jnp.concatenate([filler, tensor[: length - amount]], axis=0)


def lifted(tensor, amount):
    length = tensor.shape[0]
    amount = min(amount, length)
    filler = jnp.zeros((amount,) + tensor.shape[1:], tensor.dtype)
    return jnp.concatenate([tensor[amount:], filler], axis=0)


def local_grads(
    query_blocks,
    key_blocks,
    value_blocks,
    grad_blocks,
    far_keys,
    far_values,
    window_state,
    gain_rows,
):
    rows_iota = lax.broadcasted_iota(jnp.int32, (STRETCH, STRETCH), 0)
    cols_iota = lax.broadcasted_iota(jnp.int32, (STRETCH, STRETCH), 1)
    near_mask = rows_iota >= cols_iota
    far_mask = rows_iota < cols_iota
    near_scores = jnp.where(
        near_mask, contract("cihk,cjhk->chij", query_blocks, key_blocks), 0.0
    ).astype(jnp.bfloat16)
    far_scores = jnp.where(
        far_mask, contract("cihk,cjhk->chij", query_blocks, far_keys), 0.0
    ).astype(jnp.bfloat16)
    mixed_out = (
        contract("chij,cjhd->cihd", near_scores, value_blocks)
        + contract("chij,cjhd->cihd", far_scores, far_values)
        + contract("cihk,chkd->cihd", query_blocks, window_state)
    )
    inv_rms = lax.rsqrt(jnp.mean(mixed_out * mixed_out, axis=-1, keepdims=True) + 1e-06)
    normed = mixed_out * inv_rms
    grad_float = grad_blocks.astype(jnp.float32)
    gain_part = jnp.sum(grad_float * normed, axis=(0, 1))
    scaled = grad_float * gain_rows
    out_grad = (
        inv_rms * (scaled - normed * jnp.mean(scaled * normed, axis=-1, keepdims=True))
    ).astype(jnp.bfloat16)
    near_dscores = jnp.where(
        near_mask, contract("cihd,cjhd->chij", out_grad, value_blocks), 0.0
    ).astype(jnp.bfloat16)
    far_dscores = jnp.where(
        far_mask, contract("cihd,cjhd->chij", out_grad, far_values), 0.0
    ).astype(jnp.bfloat16)
    state_grad = contract("cihk,cihd->chkd", query_blocks, out_grad)
    query_part = (
        contract("chij,cjhk->cihk", near_dscores, key_blocks)
        + contract("chij,cjhk->cihk", far_dscores, far_keys)
        + contract("cihd,chkd->cihk", out_grad, window_state)
    )
    key_near = contract("chij,cihk->cjhk", near_dscores, query_blocks)
    key_far = contract("chij,cihk->cjhk", far_dscores, query_blocks)
    value_near = contract("chij,cihd->cjhd", near_scores, out_grad)
    value_far = contract("chij,cihd->cjhd", far_scores, out_grad)
    return (query_part, key_near, key_far, value_near, value_far, state_grad, gain_part)


def finish(
    query_part,
    key_near,
    key_far_here,
    value_near,
    value_far_here,
    key_blocks,
    value_blocks,
    kv_grad,
):
    key_part = key_near + key_far_here + contract("cjhd,chkd->cjhk", value_blocks, kv_grad)
    value_part = value_near + value_far_here + contract("cjhk,chkd->cjhd", key_blocks, kv_grad)
    return (
        query_part.astype(jnp.bfloat16),
        key_part.astype(jnp.bfloat16),
        value_part.astype(jnp.bfloat16),
    )


def blocked(tensor, heads_count):
    return tensor[0, 0].reshape(-1, STRETCH, heads_count, HEAD_DIM)


GROUP = 2
MESH = pl.DeviceIdType.MESH
NN = (((1,), (0,)), ((), ()))
NT = (((1,), (1,)), ((), ()))
TN = (((0,), (0,)), ((), ()))


def dot(left, right, dims):
    return lax.dot_general(left, right, dims, preferred_element_type=jnp.float32)


def chain_kernel(
    n_ctx,
    n_dp,
    q_ref,
    k_ref,
    v_ref,
    up_ref,
    gain_ref,
    qg_ref,
    kg_ref,
    vg_ref,
    gg_ref,
    g_buf,
    gain_all,
    gain_part,
    gain_stage,
    gain_mine,
    gain_final,
    kv_buf,
    near_buf,
    mix_buf,
    key_buf,
    val_buf,
    sg_buf,
    fwd_out,
    fwd_in,
    bwd_out,
    bwd_in,
    fwd_send,
    fwd_recv,
    bwd_send,
    bwd_recv,
    up_sem,
    gain_sem,
    stage_sem,
    final_sem,
):
    pipe = lax.axis_index("pipe")
    me = lax.axis_index("ctx")
    dp = lax.axis_index("dp")
    tokens, width = q_ref.shape
    heads = width // HEAD_DIM
    chunks = heads // GROUP
    per = width // n_ctx
    last = n_ctx - 1

    def at_ctx(c):
        return (pipe, c, dp)

    def at_dp(d):
        return (pipe, me, d)

    other = (1 - pipe, me, dp)
    ctx_peers = [lax.rem(me + o, n_ctx) for o in range(1, n_ctx)]
    dp_peers = [lax.rem(dp + o, n_dp) for o in range(1, n_dp)]

    barrier = pltpu.get_barrier_semaphore()
    pl.semaphore_signal(barrier, inc=1, device_id=other, device_id_type=MESH)
    for c in ctx_peers:
        pl.semaphore_signal(barrier, inc=1, device_id=at_ctx(c), device_id_type=MESH)
    for d in dp_peers:
        pl.semaphore_signal(barrier, inc=1, device_id=at_dp(d), device_id_type=MESH)

    def lanes(c, j):
        return pl.ds(pl.multiple_of((c * GROUP + j) * HEAD_DIM, HEAD_DIM), HEAD_DIM)

    def remote(src, dst, send, recv, target):
        return pltpu.make_async_remote_copy(
            src_ref=src,
            dst_ref=dst,
            send_sem=send,
            recv_sem=recv,
            device_id=target,
            device_id_type=MESH,
        )

    def fwd_copy(c):
        return remote(
            fwd_out.at[c],
            fwd_in.at[c],
            fwd_send.at[c],
            fwd_recv.at[c],
            at_ctx(jnp.minimum(me + 1, last)),
        )

    def bwd_copy(c):
        return remote(
            bwd_out.at[c],
            bwd_in.at[c],
            bwd_send.at[c],
            bwd_recv.at[c],
            at_ctx(jnp.maximum(me - 1, 0)),
        )

    @pl.when(me == 0)
    def _():
        fwd_in[...] = jnp.zeros_like(fwd_in)

    @pl.when(me == last)
    def _():
        bwd_in[...] = jnp.zeros_like(bwd_in)

    gain_all[me] = gain_ref[...]
    pl.semaphore_wait(barrier, 1 + len(ctx_peers) + len(dp_peers))

    def first(c, carry):
        for j in range(GROUP):
            at = lanes(c, j)
            kv = dot(k_ref[:, at], v_ref[:, at], TN)
            kv_buf[c, j] = kv
            fwd_out[c, j] = kv.astype(jnp.bfloat16)

        @pl.when(me == 0)
        def _():
            fwd_copy(c).start()

        return carry

    lax.fori_loop(0, chunks, first, 0)

    up_copy = remote(up_ref, g_buf, up_sem.at[0], up_sem.at[1], other)
    up_copy.start()
    gain_copies = []
    for o, c in enumerate(ctx_peers):
        copy = remote(
            gain_ref, gain_all.at[me], gain_sem.at[0, o], gain_sem.at[1, o], at_ctx(c)
        )
        copy.start()
        gain_copies.append(copy)

    rows = lax.broadcasted_iota(jnp.int32, (tokens, tokens), 0)
    cols = lax.broadcasted_iota(jnp.int32, (tokens, tokens), 1)
    mask = rows >= cols

    def second(c, carry):
        for j in range(GROUP):
            at = lanes(c, j)
            near = jnp.where(mask, dot(q_ref[:, at], k_ref[:, at], NT), 0.0)
            near = near.astype(jnp.bfloat16)
            near_buf[c, j] = near
            mix_buf[c, j] = dot(near, v_ref[:, at], NN)
        return carry

    lax.fori_loop(0, chunks, second, 0)

    up_copy.wait()
    for copy in gain_copies:
        copy.wait()

    def forward(c):
        @pl.when(me > 0)
        def _():
            fwd_copy(c).wait_recv()

        @pl.when(jnp.logical_and(me > 0, me < last))
        def _():
            for j in range(GROUP):
                total = kv_buf[c, j] + fwd_in[c, j].astype(jnp.float32)
                fwd_out[c, j] = total.astype(jnp.bfloat16)
            fwd_copy(c).start()

        later = []
        for j in range(GROUP):
            at = lanes(c, j)
            query, state = q_ref[:, at], fwd_in[c, j]
            mixed = mix_buf[c, j] + dot(query, state, NN)
            inv_rms = lax.rsqrt(jnp.mean(mixed * mixed, axis=-1, keepdims=True) + 1e-06)
            normed = mixed * inv_rms
            grad = g_buf[:, at].astype(jnp.float32)
            place = (c * GROUP + j) * HEAD_DIM
            owner = place // per
            inside = pl.ds(pl.multiple_of(lax.rem(place, per), HEAD_DIM), HEAD_DIM)
            product = grad * normed
            gain_part[owner, :, inside] = jnp.sum(product, axis=0, keepdims=True)
            gain_row = gain_all[owner, :, inside]
            pull = jnp.mean(product * gain_row, axis=-1, keepdims=True)
            mixed_grad = (inv_rms * (grad * gain_row - normed * pull)).astype(jnp.bfloat16)
            state_grad = dot(query, mixed_grad, TN)
            sg_buf[c, j] = state_grad
            bwd_out[c, j] = state_grad.astype(jnp.bfloat16)
            later.append((at, query, state, mixed_grad))

        @pl.when(me == last)
        def _():
            bwd_copy(c).start()

        for j, (at, query, state, mixed_grad) in enumerate(later):
            near_grad = jnp.where(mask, dot(mixed_grad, v_ref[:, at], NT), 0.0)
            near_grad = near_grad.astype(jnp.bfloat16)
            query_grad = dot(near_grad, k_ref[:, at], NN) + dot(mixed_grad, state, NT)
            qg_ref[:, at] = query_grad.astype(jnp.bfloat16)
            key_buf[c, j] = dot(near_grad, query, TN)
            val_buf[c, j] = dot(near_buf[c, j], mixed_grad, TN)

    def backward(c):
        @pl.when(me < last)
        def _():
            bwd_copy(c).wait_recv()

        @pl.when(jnp.logical_and(me > 0, me < last))
        def _():
            for j in range(GROUP):
                total = sg_buf[c, j] + bwd_in[c, j].astype(jnp.float32)
                bwd_out[c, j] = total.astype(jnp.bfloat16)
            bwd_copy(c).start()

        for j in range(GROUP):
            at = lanes(c, j)
            kv_grad = bwd_in[c, j]
            key_grad = key_buf[c, j] + dot(v_ref[:, at], kv_grad, NT)
            kg_ref[:, at] = key_grad.astype(jnp.bfloat16)
            val_grad = val_buf[c, j] + dot(k_ref[:, at], kv_grad, NN)
            vg_ref[:, at] = val_grad.astype(jnp.bfloat16)

    def stage_copy(o):
        c = ctx_peers[o]
        return remote(
            gain_part.at[c], gain_stage.at[o], stage_sem.at[0, o], stage_sem.at[1, o], at_ctx(c)
        )

    def final_copy(o):
        return remote(
            gain_mine, gain_final.at[o], final_sem.at[0, o], final_sem.at[1, o], at_dp(dp_peers[o])
        )

    lag = jnp.minimum(chunks, (last - me) * LAG)
    steps = chunks + min(chunks, last * LAG)

    def step(i, carry):
        @pl.when(i < chunks)
        def _():
            forward(i)

        @pl.when(i == chunks - 1)
        def _():
            for o in range(n_ctx - 1):
                stage_copy(o).start()

        @pl.when(i == steps - 2)
        def _():
            total = gain_part[me]
            for o in range(n_ctx - 1):
                stage_copy(o).wait()
                total = total + gain_stage[o]
            gain_mine[...] = total
            for o in range(n_dp - 1):
                final_copy(o).start()

        @pl.when(jnp.logical_and(i >= lag, i - lag < chunks))
        def _():
            backward(i - lag)

        return carry

    lax.fori_loop(0, steps, step, 0)

    total = gain_mine[...]
    for o in range(n_dp - 1):
        final_copy(o).wait()
        total = total + gain_final[o]
    gg_ref[...] = total

    @pl.when(me < last)
    def _():
        for c in range(chunks):
            fwd_copy(c).wait_send()

    @pl.when(me > 0)
    def _():
        for c in range(chunks):
            bwd_copy(c).wait_send()


LAG = 4


def chained(queries, keys, values, upstream, gain):
    n_ctx, n_dp = lax.axis_size("ctx"), lax.axis_size("dp")
    tokens, width = queries.shape[2:]
    heads = width // HEAD_DIM
    chunks = heads // GROUP
    per = gain.shape[1]
    wide = (chunks, GROUP, HEAD_DIM, HEAD_DIM)
    rows = (chunks, GROUP, tokens, HEAD_DIM)
    dma = pltpu.SemaphoreType.DMA
    vmem = pl.BlockSpec(memory_space=pltpu.VMEM)
    token_out = jax.ShapeDtypeStruct((tokens, width), jnp.bfloat16)
    flat = [x.reshape(tokens, width) for x in (queries, keys, values, upstream)]
    query_grad, key_grad, value_grad, gain_grad = pl.pallas_call(
        functools.partial(chain_kernel, n_ctx, n_dp),
        out_shape=(token_out, token_out, token_out, jax.ShapeDtypeStruct((1, per), jnp.float32)),
        in_specs=[vmem] * 5,
        out_specs=(vmem,) * 4,
        scratch_shapes=[
            pltpu.VMEM((tokens, width), jnp.bfloat16),
            pltpu.VMEM((n_ctx, 1, per), jnp.float32),
            pltpu.VMEM((n_ctx, 1, per), jnp.float32),
            pltpu.VMEM((n_ctx, 1, per), jnp.float32),
            pltpu.VMEM((1, per), jnp.float32),
            pltpu.VMEM((n_dp, 1, per), jnp.float32),
            pltpu.VMEM(wide, jnp.float32),
            pltpu.VMEM((chunks, GROUP, tokens, tokens), jnp.bfloat16),
            pltpu.VMEM(rows, jnp.float32),
            pltpu.VMEM(rows, jnp.float32),
            pltpu.VMEM(rows, jnp.float32),
            pltpu.VMEM(wide, jnp.float32),
            pltpu.VMEM(wide, jnp.bfloat16),
            pltpu.VMEM(wide, jnp.bfloat16),
            pltpu.VMEM(wide, jnp.bfloat16),
            pltpu.VMEM(wide, jnp.bfloat16),
            dma((chunks,)),
            dma((chunks,)),
            dma((chunks,)),
            dma((chunks,)),
            dma((2,)),
            dma((2, n_ctx)),
            dma((2, n_ctx)),
            dma((2, n_dp)),
        ],
        compiler_params=pltpu.CompilerParams(
            collective_id=0, has_side_effects=True, vmem_limit_bytes=40 * 1024 * 1024
        ),
    )(*flat, gain)
    shape = queries.shape
    return (
        query_grad.reshape(shape),
        key_grad.reshape(shape),
        value_grad.reshape(shape),
        gain_grad,
    )


def shards(queries, keys, values, upstream, gain):
    reach_blocks = WINDOW // STRETCH
    if (
        queries.shape[2] == STRETCH
        and 1 < lax.axis_size("ctx") <= reach_blocks
        and lax.axis_size("pipe") == 2
    ):
        return chained(queries, keys, values, upstream, gain)
    incoming = shifted_2(upstream, "pipe", -1)
    heads_here = gain.shape[1] // HEAD_DIM
    query_heads, key_heads, value_heads, grad_heads = (
        lax.all_to_all(queries, "ctx", split_axis=3, concat_axis=2, tiled=True),
        lax.all_to_all(keys, "ctx", split_axis=3, concat_axis=2, tiled=True),
        lax.all_to_all(values, "ctx", split_axis=3, concat_axis=2, tiled=True),
        lax.all_to_all(incoming, "ctx", split_axis=3, concat_axis=2, tiled=True),
    )
    seq_len = query_heads.shape[2]
    gain_rows = gain[0].reshape(heads_here, HEAD_DIM)
    query_blocks = blocked(query_heads, heads_here)
    key_blocks = blocked(key_heads, heads_here)
    value_blocks = blocked(value_heads, heads_here)
    grad_blocks = blocked(grad_heads, heads_here)
    kv_stretches = contract("cshi,cshj->chij", key_blocks, value_blocks)
    prefix = shifted(jnp.cumsum(kv_stretches, axis=0), 1)
    window_state = (prefix - shifted(prefix, reach_blocks - 1)).astype(jnp.bfloat16)
    far_keys = shifted(key_blocks, reach_blocks)
    far_values = shifted(value_blocks, reach_blocks)
    query_part, key_near, key_far, value_near, value_far, state_grad, gain_part = local_grads(
        query_blocks,
        key_blocks,
        value_blocks,
        grad_blocks,
        far_keys,
        far_values,
        window_state,
        gain_rows,
    )
    later = lifted(jnp.flip(jnp.cumsum(jnp.flip(state_grad, 0), axis=0), 0), 1)
    kv_grad = (later - lifted(later, reach_blocks - 1)).astype(jnp.bfloat16)
    query_out, key_out, value_out = finish(
        query_part,
        key_near,
        lifted(key_far, reach_blocks),
        value_near,
        lifted(value_far, reach_blocks),
        key_blocks,
        value_blocks,
        kv_grad,
    )

    def head_rows(tensor):
        return tensor.reshape(1, 1, seq_len, heads_here * HEAD_DIM)

    query_grad, key_grad, value_grad = (
        lax.all_to_all(head_rows(query_out), "ctx", split_axis=2, concat_axis=3, tiled=True),
        lax.all_to_all(head_rows(key_out), "ctx", split_axis=2, concat_axis=3, tiled=True),
        lax.all_to_all(head_rows(value_out), "ctx", split_axis=2, concat_axis=3, tiled=True),
    )
    gain_share = gain_part.reshape(1, heads_here * HEAD_DIM)
    gain_total = lax.psum(gain_share, "dp")
    return (query_grad, key_grad, value_grad, gain_total)


def solution(mesh):
    in_specs = (
        P("pipe", "dp", "ctx", None),
        P("pipe", "dp", "ctx", None),
        P("pipe", "dp", "ctx", None),
        P("pipe", "dp", "ctx", None),
        P("pipe", "ctx"),
    )
    out_specs = (
        P("pipe", "dp", "ctx", None),
        P("pipe", "dp", "ctx", None),
        P("pipe", "dp", "ctx", None),
        P("pipe", "ctx"),
    )
    return jax.shard_map(shards, mesh=mesh, in_specs=in_specs, out_specs=out_specs, check_vma=False)
```

profile of v0, /device:TPU:0, one launch (start us, length us, event | category | flops | bytes accessed | tf_op | source)
XLA Modules:
  0.0 56.9 jit_solution(7087150049630656134)
XLA Ops:
  0.6 0.0 copy-start.4
  0.6 0.7 %copy-done.4 = f32[1,512]{1,0:T(1,128)S(1)} copy-done((f32[1,512]{1,0:T(1,128)S(1)}, f32[1,512]{1,0:T(1,128)}, u32[]{:S(2)}) %copy-start.4) | copy-done | bytes 2072
  1.3 0.0 copy-start
  1.3 1.0 %copy-done = bf16[1,1,128,2048]{3,2,1,0:T(8,128)(2,1)S(1)} copy-done((bf16[1,1,128,2048]{3,2,1,0:T(8,128)(2,1)S(1)}, bf16[1,1,128,2048]{3,2,1,0:T(8,128)(2,1)}, u32[]{:S(2)}) %copy-start) | copy-done | bytes 524312
  2.4 0.0 copy-start.1
  2.4 1.0 %copy-done.1 = bf16[1,1,128,2048]{3,2,1,0:T(8,128)(2,1)S(1)} copy-done((bf16[1,1,128,2048]{3,2,1,0:T(8,128)(2,1)S(1)}, bf16[1,1,128,2048]{3,2,1,0:T(8,128)(2,1)}, u32[]{:S(2)}) %copy-start.1) | copy-done | bytes 524312
  3.4 0.0 copy-start.2
  3.4 1.0 %copy-done.2 = bf16[1,1,128,2048]{3,2,1,0:T(8,128)(2,1)S(1)} copy-done((bf16[1,1,128,2048]{3,2,1,0:T(8,128)(2,1)S(1)}, bf16[1,1,128,2048]{3,2,1,0:T(8,128)(2,1)}, u32[]{:S(2)}) %copy-start.2) | copy-done | bytes 524312
  4.4 0.0 copy-start.3
  4.4 1.0 %copy-done.3 = bf16[1,1,128,2048]{3,2,1,0:T(8,128)(2,1)S(1)} copy-done((bf16[1,1,128,2048]{3,2,1,0:T(8,128)(2,1)S(1)}, bf16[1,1,128,2048]{3,2,1,0:T(8,128)(2,1)}, u32[]{:S(2)}) %copy-start.3) | copy-done | bytes 524312
  5.5 48.4 %shard_map.84 = (bf16[128,2048]{1,0:T(8,128)(2,1)S(1)}, bf16[128,2048]{1,0:T(8,128)(2,1)S(1)}, bf16[128,2048]{1,0:T(8,128)(2,1)S(1)}, f32[1,512]{1,0:T(1,128)S(1)}) custom-call(bf16[128,2048]{1,0:T(8,128)(2,1)S(1)} %bitcast.7, bf16[128,2048]{1,0:T(8,128)(2,1)S(1)} %bitcast.8, bf16[128,2048]{1,0:T(8,128)(2,1)S(1)} %bitcast.9, bf16[128,2048]{1,0:T(8,128)(2,1)S(1)} %bitcast.10, ...), custom_call_target="tpu_custom_call" | custom-call | tf_op jit(solution)/shard_map/pallas_call | solution.py:412
  53.9 0.8 %copy.13 = bf16[1,1,128,2048]{3,2,1,0:T(8,128)(2,1)} copy(bf16[1,1,128,2048]{3,2,1,0:T(8,128)(2,1)S(1)} %bitcast.13) | data formatting | bytes 1048576
  54.7 0.8 %copy.14 = bf16[1,1,128,2048]{3,2,1,0:T(8,128)(2,1)} copy(bf16[1,1,128,2048]{3,2,1,0:T(8,128)(2,1)S(1)} %bitcast.12) | data formatting | bytes 1048576
  55.5 0.8 %copy.15 = bf16[1,1,128,2048]{3,2,1,0:T(8,128)(2,1)} copy(bf16[1,1,128,2048]{3,2,1,0:T(8,128)(2,1)S(1)} %bitcast.11) | data formatting | bytes 1048576
  56.3 0.6 %copy.16 = f32[1,512]{1,0:T(1,128)} copy(f32[1,512]{1,0:T(1,128)S(1)} %get-tuple-element.19) | data formatting | bytes 4096
Async XLA Ops:
  0.6 0.7 %copy-start.4 = (f32[1,512]{1,0:T(1,128)S(1)}, f32[1,512]{1,0:T(1,128)}, u32[]{:S(2)}) copy-start(f32[1,512]{1,0:T(1,128)} %gain_ref.1) | copy-start | bytes 6148
  1.3 1.0 %copy-start = (bf16[1,1,128,2048]{3,2,1,0:T(8,128)(2,1)S(1)}, bf16[1,1,128,2048]{3,2,1,0:T(8,128)(2,1)}, u32[]{:S(2)}) copy-start(bf16[1,1,128,2048]{3,2,1,0:T(8,128)(2,1)} %param.5) | copy-start | bytes 1572868
  2.4 1.0 %copy-start.1 = (bf16[1,1,128,2048]{3,2,1,0:T(8,128)(2,1)S(1)}, bf16[1,1,128,2048]{3,2,1,0:T(8,128)(2,1)}, u32[]{:S(2)}) copy-start(bf16[1,1,128,2048]{3,2,1,0:T(8,128)(2,1)} %param.6) | copy-start | bytes 1572868
  3.4 1.0 %copy-start.2 = (bf16[1,1,128,2048]{3,2,1,0:T(8,128)(2,1)S(1)}, bf16[1,1,128,2048]{3,2,1,0:T(8,128)(2,1)}, u32[]{:S(2)}) copy-start(bf16[1,1,128,2048]{3,2,1,0:T(8,128)(2,1)} %param.7) | copy-start | bytes 1572868
  4.4 1.0 %copy-start.3 = (bf16[1,1,128,2048]{3,2,1,0:T(8,128)(2,1)S(1)}, bf16[1,1,128,2048]{3,2,1,0:T(8,128)(2,1)}, u32[]{:S(2)}) copy-start(bf16[1,1,128,2048]{3,2,1,0:T(8,128)(2,1)} %param.8) | copy-start | bytes 1572868
where the time goes:
time: 57.2 us; the launch traced here: 56.9 us
  Pallas kernels  48.4 us (85%)
  local copies, waits for them, and re-layouts  7.8 us (14%)
  between operations  0.65 us (1%)
    pallas_call x1, Pallas kernels, chained(): pl.pallas_call(functools.partial(chain_kernel, n_ctx, n_dp), out_shape=(t...  48.4 us
    unnamed x14, local copies, waits for them, and re-layouts  7.8 us

commit v1 on v0

--- a/solution.py
+++ b/solution.py
@@ -124,15 +124,21 @@
 def chain_kernel(
     n_ctx,
     n_dp,
+    q_hbm,
+    k_hbm,
+    v_hbm,
+    up_ref,
+    gain_ref,
+    qg_hbm,
+    kg_hbm,
+    vg_hbm,
+    gg_ref,
+    qg_ref,
+    kg_ref,
+    vg_ref,
     q_ref,
     k_ref,
     v_ref,
-    up_ref,
-    gain_ref,
-    qg_ref,
-    kg_ref,
-    vg_ref,
-    gg_ref,
     g_buf,
     gain_all,
     gain_part,
@@ -153,11 +159,19 @@
     fwd_recv,
     bwd_send,
     bwd_recv,
+    load_sem,
+    store_sem,
     up_sem,
     gain_sem,
     stage_sem,
     final_sem,
 ):
+    loads = [
+        pltpu.make_async_copy(src, dst, load_sem.at[i])
+        for i, (src, dst) in enumerate(((k_hbm, k_ref), (v_hbm, v_ref), (q_hbm, q_ref)))
+    ]
+    for load in loads:
+        load.start()
     pipe = lax.axis_index("pipe")
     me = lax.axis_index("ctx")
     dp = lax.axis_index("dp")
@@ -197,21 +211,21 @@
             device_id_type=MESH,
         )
 
-    def fwd_copy(c):
+    def fwd_copy(c, j):
         return remote(
-            fwd_out.at[c],
-            fwd_in.at[c],
-            fwd_send.at[c],
-            fwd_recv.at[c],
+            fwd_out.at[c, j],
+            fwd_in.at[c, j],
+            fwd_send.at[c, j],
+            fwd_recv.at[c, j],
             at_ctx(jnp.minimum(me + 1, last)),
         )
 
-    def bwd_copy(c):
+    def bwd_copy(c, j):
         return remote(
-            bwd_out.at[c],
-            bwd_in.at[c],
-            bwd_send.at[c],
-            bwd_recv.at[c],
+            bwd_out.at[c, j],
+            bwd_in.at[c, j],
+            bwd_send.at[c, j],
+            bwd_recv.at[c, j],
             at_ctx(jnp.maximum(me - 1, 0)),
         )
 
@@ -223,7 +237,10 @@
     def _():
         bwd_in[...] = jnp.zeros_like(bwd_in)
 
-    gain_all[me] = gain_ref[...]
+    own_gain = pltpu.make_async_copy(gain_ref, gain_all.at[me], load_sem.at[3])
+    own_gain.start()
+    loads[0].wait()
+    loads[1].wait()
     pl.semaphore_wait(barrier, 1 + len(ctx_peers) + len(dp_peers))
 
     def first(c, carry):
@@ -235,7 +252,8 @@
 
         @pl.when(me == 0)
         def _():
-            fwd_copy(c).start()
+            for j in range(GROUP):
+                fwd_copy(c, j).start()
 
         return carry
 
@@ -251,6 +269,8 @@
         copy.start()
         gain_copies.append(copy)
 
+    loads[2].wait()
+    own_gain.wait()
     rows = lax.broadcasted_iota(jnp.int32, (tokens, tokens), 0)
     cols = lax.broadcasted_iota(jnp.int32, (tokens, tokens), 1)
     mask = rows >= cols
@@ -270,17 +290,26 @@
     for copy in gain_copies:
         copy.wait()
 
+    def store(which, c):
+        source = (qg_ref, kg_ref, vg_ref)[which]
+        target = (qg_hbm, kg_hbm, vg_hbm)[which]
+        wide = GROUP * HEAD_DIM
+        at = pl.ds(pl.multiple_of(c * wide, wide), wide)
+        return pltpu.make_async_copy(source.at[:, at], target.at[:, at], store_sem.at[which, c])
+
     def forward(c):
-        @pl.when(me > 0)
-        def _():
-            fwd_copy(c).wait_recv()
+        @pl.when(me == last)
+        def _():
+            for j in range(GROUP):
+                fwd_copy(c, j).wait_recv()
 
         @pl.when(jnp.logical_and(me > 0, me < last))
         def _():
             for j in range(GROUP):
+                fwd_copy(c, j).wait_recv()
                 total = kv_buf[c, j] + fwd_in[c, j].astype(jnp.float32)
                 fwd_out[c, j] = total.astype(jnp.bfloat16)
-            fwd_copy(c).start()
+                fwd_copy(c, j).start()
 
         later = []
         for j in range(GROUP):
@@ -305,7 +334,8 @@
 
         @pl.when(me == last)
         def _():
-            bwd_copy(c).start()
+            for j in range(GROUP):
+                bwd_copy(c, j).start()
 
         for j, (at, query, state, mixed_grad) in enumerate(later):
             near_grad = jnp.where(mask, dot(mixed_grad, v_ref[:, at], NT), 0.0)
@@ -314,18 +344,21 @@
             qg_ref[:, at] = query_grad.astype(jnp.bfloat16)
             key_buf[c, j] = dot(near_grad, query, TN)
             val_buf[c, j] = dot(near_buf[c, j], mixed_grad, TN)
+        store(0, c).start()
 
     def backward(c):
-        @pl.when(me < last)
-        def _():
-            bwd_copy(c).wait_recv()
+        @pl.when(me == 0)
+        def _():
+            for j in range(GROUP):
+                bwd_copy(c, j).wait_recv()
 
         @pl.when(jnp.logical_and(me > 0, me < last))
         def _():
             for j in range(GROUP):
+                bwd_copy(c, j).wait_recv()
                 total = sg_buf[c, j] + bwd_in[c, j].astype(jnp.float32)
                 bwd_out[c, j] = total.astype(jnp.bfloat16)
-            bwd_copy(c).start()
+                bwd_copy(c, j).start()
 
         for j in range(GROUP):
             at = lanes(c, j)
@@ -334,6 +367,8 @@
             kg_ref[:, at] = key_grad.astype(jnp.bfloat16)
             val_grad = val_buf[c, j] + dot(k_ref[:, at], kv_grad, NN)
             vg_ref[:, at] = val_grad.astype(jnp.bfloat16)
+        store(1, c).start()
+        store(2, c).start()
 
     def stage_copy(o):
         c = ctx_peers[o]
@@ -359,7 +394,7 @@
             for o in range(n_ctx - 1):
                 stage_copy(o).start()
 
-        @pl.when(i == steps - 2)
+        @pl.when(i == steps - 3)
         def _():
             total = gain_part[me]
             for o in range(n_ctx - 1):
@@ -381,20 +416,50 @@
     for o in range(n_dp - 1):
         final_copy(o).wait()
         total = total + gain_final[o]
-    gg_ref[...] = total
+    gain_mine[...] = total
+    out_gain = pltpu.make_async_copy(gain_mine, gg_ref, load_sem.at[4])
+    out_gain.start()
+    for c in range(chunks):
+        for which in range(3):
+            store(which, c).wait()
+    out_gain.wait()
 
     @pl.when(me < last)
     def _():
         for c in range(chunks):
-            fwd_copy(c).wait_send()
+            for j in range(GROUP):
+                fwd_copy(c, j).wait_send()
 
     @pl.when(me > 0)
     def _():
         for c in range(chunks):
-            bwd_copy(c).wait_send()
+            for j in range(GROUP):
+                bwd_copy(c, j).wait_send()
 
 
 LAG = 4
+VMEM_BYTES = 63 * 1024 * 1024
+PIECES = 4
+
+
+def store_kernel(*refs):
+    sources, targets, held, in_sems, out_sems = refs[:4], refs[4:8], refs[8:12], refs[12], refs[13]
+    inward, outward = [], []
+    for i in range(4):
+        rows = sources[i].shape[0]
+        pieces = PIECES if rows % (16 * PIECES) == 0 else 1
+        for p in range(pieces):
+            at = pl.ds(p * (rows // pieces), rows // pieces)
+            here = held[i].at[at]
+            inward.append(pltpu.make_async_copy(sources[i].at[at], here, in_sems.at[i, p]))
+            outward.append(pltpu.make_async_copy(here, targets[i].at[at], out_sems.at[i, p]))
+    for copy in inward:
+        copy.start()
+    for arrived, copy in zip(inward, outward):
+        arrived.wait()
+        copy.start()
+    for copy in outward:
+        copy.wait()
 
 
 def chained(queries, keys, values, upstream, gain):
@@ -406,15 +471,22 @@
     wide = (chunks, GROUP, HEAD_DIM, HEAD_DIM)
     rows = (chunks, GROUP, tokens, HEAD_DIM)
     dma = pltpu.SemaphoreType.DMA
-    vmem = pl.BlockSpec(memory_space=pltpu.VMEM)
     token_out = jax.ShapeDtypeStruct((tokens, width), jnp.bfloat16)
     flat = [x.reshape(tokens, width) for x in (queries, keys, values, upstream)]
-    query_grad, key_grad, value_grad, gain_grad = pl.pallas_call(
+    hbm = pl.BlockSpec(memory_space=pltpu.HBM)
+    shapes = (token_out, token_out, token_out, jax.ShapeDtypeStruct((1, per), jnp.float32))
+    grads = pl.pallas_call(
         functools.partial(chain_kernel, n_ctx, n_dp),
-        out_shape=(token_out, token_out, token_out, jax.ShapeDtypeStruct((1, per), jnp.float32)),
-        in_specs=[vmem] * 5,
-        out_specs=(vmem,) * 4,
+        out_shape=shapes,
+        in_specs=[hbm] * 5,
+        out_specs=(hbm,) * 4,
         scratch_shapes=[
+            pltpu.VMEM((tokens, width), jnp.bfloat16),
+            pltpu.VMEM((tokens, width), jnp.bfloat16),
+            pltpu.VMEM((tokens, width), jnp.bfloat16),
+            pltpu.VMEM((tokens, width), jnp.bfloat16),
+            pltpu.VMEM((tokens, width), jnp.bfloat16),
+            pltpu.VMEM((tokens, width), jnp.bfloat16),
             pltpu.VMEM((tokens, width), jnp.bfloat16),
             pltpu.VMEM((n_ctx, 1, per), jnp.float32),
             pltpu.VMEM((n_ctx, 1, per), jnp.float32),
@@ -431,19 +503,30 @@
             pltpu.VMEM(wide, jnp.bfloat16),
             pltpu.VMEM(wide, jnp.bfloat16),
             pltpu.VMEM(wide, jnp.bfloat16),
-            dma((chunks,)),
-            dma((chunks,)),
-            dma((chunks,)),
-            dma((chunks,)),
+            dma((chunks, GROUP)),
+            dma((chunks, GROUP)),
+            dma((chunks, GROUP)),
+            dma((chunks, GROUP)),
+            dma((5,)),
+            dma((3, chunks)),
             dma((2,)),
             dma((2, n_ctx)),
             dma((2, n_ctx)),
             dma((2, n_dp)),
         ],
         compiler_params=pltpu.CompilerParams(
-            collective_id=0, has_side_effects=True, vmem_limit_bytes=40 * 1024 * 1024
+            collective_id=0, has_side_effects=True, vmem_limit_bytes=VMEM_BYTES
         ),
     )(*flat, gain)
+    query_grad, key_grad, value_grad, gain_grad = pl.pallas_call(
+        store_kernel,
+        out_shape=shapes,
+        in_specs=[hbm] * 4,
+        out_specs=(hbm,) * 4,
+        scratch_shapes=[pltpu.VMEM(x.shape, x.dtype) for x in shapes]
+        + [dma((4, PIECES)), dma((4, PIECES))],
+        compiler_params=pltpu.CompilerParams(vmem_limit_bytes=VMEM_BYTES),
+    )(*grads)
     shape = queries.shape
     return (
         query_grad.reshape(shape),

time: 57.2 us -> 51 us (0.89)
  local copies, waits for them, and re-layouts: 7.8 us -> 0 us
  Pallas kernels: 48.4 us -> 50.2 us
    unnamed x14 -> x0, local copies, waits for them, and re-layouts: 7.8 us -> none
    pallas_call x1 -> x2, Pallas kernels: 48.4 us -> 50.2 us  [the longest x1 47.8 us: chained(): pl.pallas_call(functools.partial(chain_kernel, n_ctx, n_dp), out_shape=sh...]
where the time goes in v1:
time: 51 us; the launch traced here: 50.8 us
  Pallas kernels  50.2 us (98%)
  between operations  0.64 us (1%)
    pallas_call x1, Pallas kernels, chained(): pl.pallas_call(functools.partial(chain_kernel, n_ctx, n_dp), out_shape=sh...  47.8 us
    pallas_call x1, Pallas kernels, chained(): pl.pallas_call(store_kernel, out_shape=shapes, in_specs=[hbm] * 4, out_sp...  2.4 us

profile of v1, /device:TPU:0, one launch (start us, length us, event | category | flops | bytes accessed | tf_op | source)
XLA Modules:
  0.0 50.8 jit_solution(6913466338767912415)
XLA Ops:
  0.6 47.8 %shard_map.84 = (bf16[128,2048]{1,0:T(8,128)(2,1)}, bf16[128,2048]{1,0:T(8,128)(2,1)}, bf16[128,2048]{1,0:T(8,128)(2,1)}, f32[1,512]{1,0:T(1,128)}) custom-call(bf16[128,2048]{1,0:T(8,128)(2,1)} %bitcast.7, bf16[128,2048]{1,0:T(8,128)(2,1)} %bitcast.8, bf16[128,2048]{1,0:T(8,128)(2,1)} %bitcast.9, bf16[128,2048]{1,0:T(8,128)(2,1)} %bitcast.10, f32[1,512]{1,0:T(1,128)} %gain_ref.1), custom_call_target="tpu_custom_call" | custom-call | tf_op jit(solution)/shard_map/pallas_call | solution.py:478
  48.4 2.4 %shard_map.85 = (bf16[128,2048]{1,0:T(8,128)(2,1)}, bf16[128,2048]{1,0:T(8,128)(2,1)}, bf16[128,2048]{1,0:T(8,128)(2,1)}, f32[1,512]{1,0:T(1,128)}) custom-call(bf16[128,2048]{1,0:T(8,128)(2,1)} %get-tuple-element.12.refs_0_, bf16[128,2048]{1,0:T(8,128)(2,1)} %get-tuple-element.13.refs_1_, bf16[128,2048]{1,0:T(8,128)(2,1)} %get-tuple-element.14.refs_2_, ...), custom_call_target="tpu_custom_call" | custom-call | tf_op jit(solution)/shard_map/pallas_call | solution.py:521

commit v2 on v1

--- a/solution.py
+++ b/solution.py
@@ -253,11 +253,15 @@
         @pl.when(me == 0)
         def _():
             for j in range(GROUP):
+                before = jnp.maximum(c * GROUP + j - DEPTH, 0)
+
+                @pl.when(c * GROUP + j >= DEPTH)
+                def _():
+                    fwd_copy(before // GROUP, lax.rem(before, GROUP)).wait_send()
+
                 fwd_copy(c, j).start()
 
         return carry
-
-    lax.fori_loop(0, chunks, first, 0)
 
     up_copy = remote(up_ref, g_buf, up_sem.at[0], up_sem.at[1], other)
     up_copy.start()
@@ -268,6 +272,8 @@
         )
         copy.start()
         gain_copies.append(copy)
+
+    lax.fori_loop(0, chunks, first, 0)
 
     loads[2].wait()
     own_gain.wait()
@@ -426,9 +432,13 @@
 
     @pl.when(me < last)
     def _():
-        for c in range(chunks):
-            for j in range(GROUP):
-                fwd_copy(c, j).wait_send()
+        for h in range(max(heads - DEPTH, 0), heads):
+            fwd_copy(h // GROUP, h % GROUP).wait_send()
+
+    @pl.when(jnp.logical_and(me > 0, me < last))
+    def _():
+        for h in range(heads - DEPTH):
+            fwd_copy(h // GROUP, h % GROUP).wait_send()
 
     @pl.when(me > 0)
     def _():
@@ -438,6 +448,7 @@
 
 
 LAG = 4
+DEPTH = 3
 VMEM_BYTES = 63 * 1024 * 1024
 PIECES = 4
 

time: 51 us -> 43.2 us (0.85)
  Pallas kernels: 50.2 us -> 42.4 us
    pallas_call x1, Pallas kernels: 47.8 us -> 40 us  [chained(): pl.pallas_call(functools.partial(chain_kernel, n_ctx, n_dp), out_shape=sh...]
where the time goes in v2:
time: 43.2 us; the launch traced here: 43 us
  Pallas kernels  42.4 us (98%)
  between operations  0.64 us (1%)
    pallas_call x1, Pallas kernels, chained(): pl.pallas_call(functools.partial(chain_kernel, n_ctx, n_dp), out_shape=sh...  40 us
    pallas_call x1, Pallas kernels, chained(): pl.pallas_call(store_kernel, out_shape=shapes, in_specs=[hbm] * 4, out_sp...  2.4 us

profile of v2, /device:TPU:0, one launch (start us, length us, event | category | flops | bytes accessed | tf_op | source)
XLA Modules:
  0.0 43.0 jit_solution(14273376686730949547)
XLA Ops:
  0.6 40.0 %shard_map.84 = (bf16[128,2048]{1,0:T(8,128)(2,1)}, bf16[128,2048]{1,0:T(8,128)(2,1)}, bf16[128,2048]{1,0:T(8,128)(2,1)}, f32[1,512]{1,0:T(1,128)}) custom-call(bf16[128,2048]{1,0:T(8,128)(2,1)} %bitcast.7, bf16[128,2048]{1,0:T(8,128)(2,1)} %bitcast.8, bf16[128,2048]{1,0:T(8,128)(2,1)} %bitcast.9, bf16[128,2048]{1,0:T(8,128)(2,1)} %bitcast.10, f32[1,512]{1,0:T(1,128)} %gain_ref.1), custom_call_target="tpu_custom_call" | custom-call | tf_op jit(solution)/shard_map/pallas_call | solution.py:489
  40.6 2.4 %shard_map.85 = (bf16[128,2048]{1,0:T(8,128)(2,1)}, bf16[128,2048]{1,0:T(8,128)(2,1)}, bf16[128,2048]{1,0:T(8,128)(2,1)}, f32[1,512]{1,0:T(1,128)}) custom-call(bf16[128,2048]{1,0:T(8,128)(2,1)} %get-tuple-element.12.refs_0_, bf16[128,2048]{1,0:T(8,128)(2,1)} %get-tuple-element.13.refs_1_, bf16[128,2048]{1,0:T(8,128)(2,1)} %get-tuple-element.14.refs_2_, ...), custom_call_target="tpu_custom_call" | custom-call | tf_op jit(solution)/shard_map/pallas_call | solution.py:532

commit v3 on v2

--- a/solution.py
+++ b/solution.py
@@ -241,7 +241,6 @@
     own_gain.start()
     loads[0].wait()
     loads[1].wait()
-    pl.semaphore_wait(barrier, 1 + len(ctx_peers) + len(dp_peers))
 
     def first(c, carry):
         for j in range(GROUP):
@@ -249,7 +248,12 @@
             kv = dot(k_ref[:, at], v_ref[:, at], TN)
             kv_buf[c, j] = kv
             fwd_out[c, j] = kv.astype(jnp.bfloat16)
-
+        return carry
+
+    lax.fori_loop(0, chunks, first, 0)
+    pl.semaphore_wait(barrier, 1 + len(ctx_peers) + len(dp_peers))
+
+    def launch(c, carry):
         @pl.when(me == 0)
         def _():
             for j in range(GROUP):
@@ -273,7 +277,7 @@
         copy.start()
         gain_copies.append(copy)
 
-    lax.fori_loop(0, chunks, first, 0)
+    lax.fori_loop(0, chunks, launch, 0)
 
     loads[2].wait()
     own_gain.wait()
@@ -450,7 +454,7 @@
 LAG = 4
 DEPTH = 3
 VMEM_BYTES = 63 * 1024 * 1024
-PIECES = 4
+PIECES = 2
 
 
 def store_kernel(*refs):

time: 43.2 us -> 42.2 us (0.977)
  Pallas kernels: 42.4 us -> 41.4 us
    pallas_call x1, Pallas kernels: 40 us -> 39.2 us  [chained(): pl.pallas_call(functools.partial(chain_kernel, n_ctx, n_dp), out_shape=sh...]
where the time goes in v3:
time: 42.2 us; the launch traced here: 42.1 us
  Pallas kernels  41.4 us (98%)
  between operations  0.64 us (2%)
    pallas_call x1, Pallas kernels, chained(): pl.pallas_call(functools.partial(chain_kernel, n_ctx, n_dp), out_shape=sh...  39.2 us
    pallas_call x1, Pallas kernels, chained(): pl.pallas_call(store_kernel, out_shape=shapes, in_specs=[hbm] * 4, out_sp...  2.23 us

profile of v3, /device:TPU:0, one launch (start us, length us, event | category | flops | bytes accessed | tf_op | source)
XLA Modules:
  0.0 42.1 jit_solution(5447681387677513259)
XLA Ops:
  0.6 39.2 %shard_map.84 = (bf16[128,2048]{1,0:T(8,128)(2,1)}, bf16[128,2048]{1,0:T(8,128)(2,1)}, bf16[128,2048]{1,0:T(8,128)(2,1)}, f32[1,512]{1,0:T(1,128)}) custom-call(bf16[128,2048]{1,0:T(8,128)(2,1)} %bitcast.7, bf16[128,2048]{1,0:T(8,128)(2,1)} %bitcast.8, bf16[128,2048]{1,0:T(8,128)(2,1)} %bitcast.9, bf16[128,2048]{1,0:T(8,128)(2,1)} %bitcast.10, f32[1,512]{1,0:T(1,128)} %gain_ref.1), custom_call_target="tpu_custom_call" | custom-call | tf_op jit(solution)/shard_map/pallas_call | solution.py:493
  39.8 2.2 %shard_map.85 = (bf16[128,2048]{1,0:T(8,128)(2,1)}, bf16[128,2048]{1,0:T(8,128)(2,1)}, bf16[128,2048]{1,0:T(8,128)(2,1)}, f32[1,512]{1,0:T(1,128)}) custom-call(bf16[128,2048]{1,0:T(8,128)(2,1)} %get-tuple-element.12.refs_0_, bf16[128,2048]{1,0:T(8,128)(2,1)} %get-tuple-element.13.refs_1_, bf16[128,2048]{1,0:T(8,128)(2,1)} %get-tuple-element.14.refs_2_, ...), custom_call_target="tpu_custom_call" | custom-call | tf_op jit(solution)/shard_map/pallas_call | solution.py:536
